TPU v7x, 32 devices: a whole 2x2x4 slice. The times are simulated.
32 devices in a mesh: node: 4 (over y, core), fsdp: 8 (over z, x).
Axes of the slice: x: 2, y: 2, z: 4, core: 2. Of those that a mesh axis runs over, the one named last changes fastest.
Arguments:
- activations: bfloat16 [32768, 2560], P(('node', 'fsdp'))
- grad_out: bfloat16 [32768, 2560], P(('node', 'fsdp'))
Outputs:
- combined: float32 [2560, 2560], P('fsdp', 'node')
All inputs are finite; a program needn't handle non-finite values.
Results may differ from a plain program's by a relative error of at most 0.0003.
Values may be sent and summed in bfloat16 or wider, within the bound.
A program may use at most 256 MiB of HBM per device.

v0:
```python
import jax
import jax.numpy as jnp
from jax import lax
from jax.sharding import PartitionSpec as P

EPS = 1e-06


def partner(array, axis, distance):
    return lax.ppermute(array, axis, [(i, i ^ 1 << distance) for i in range(lax.axis_size(axis))])


def group_totals(sums, node_index, bit, node_count):
    slot = node_index % 2**bit
    selector = (jnp.arange(node_count) == slot).astype(jnp.float32)
    spread = sums[:, None] * selector[None, :]
    totals = lax.psum(spread, ("node", "fsdp"))
    return jnp.sum(totals * selector[None, :], axis=1)


def local(activations, grad_out):
    node_count = lax.axis_size("node")
    current = lax.psum_scatter(
        lax.dot_general(
            activations, grad_out, (((0,), (0,)), ((), ())), preferred_element_type=jnp.float32
        ),
        "fsdp",
        scatter_dimension=0,
        tiled=True,
    )
    node_index = lax.axis_index("node")
    levels = node_count.bit_length() - 1
    for level in range(levels):
        bit = levels - 1 - level
        upper = node_index // 2**bit % 2
        half = current.shape[1] // 2
        lower_part = current[:, :half]
        upper_part = current[:, half:]
        keep = jnp.where(upper == 0, lower_part, upper_part)
        give = jnp.where(upper == 0, upper_part, lower_part)
        arrived = partner(give, "node", bit)
        first = jnp.where(upper == 0, keep, arrived)
        second = jnp.where(upper == 0, arrived, keep)
        sums = jnp.stack(
            [jnp.sum(first * second), jnp.sum(first * first), jnp.sum(second * second)]
        )
        totals = group_totals(sums, node_index, bit, node_count)
        coef_first = 1.0 - totals[0] / (2.0 * (totals[1] + EPS))
        coef_second = 1.0 - totals[0] / (2.0 * (totals[2] + EPS))
        current = coef_first * first + coef_second * second
    return current


def solution(mesh):
    in_specs = (P(("node", "fsdp"), None), P(("node", "fsdp"), None))
    out_specs = P("fsdp", "node")
    return jax.shard_map(local, mesh=mesh, in_specs=in_specs, out_specs=out_specs, check_vma=False)
```

profile of v0, /device:TPU:0, one launch (start us, length us, event | category | flops | bytes accessed | tf_op | source)
XLA Modules:
  0.0 599.0 jit_solution(2876108566160168770)
XLA Ops:
  6.5 0.0 reduce-scatter.2.cloned.1.call-start
  6.5 22.2 %fusion.2 = f32[2560,2560]{1,0:T(8,128)} fusion(bf16[1024,2560]{1,0:T(8,128)(2,1)} %param.2, bf16[1024,2560]{1,0:T(8,128)(2,1)} %param.3), kind=kOutput, calls=%fused_computation.26 | convolution fusion | flops 13421772800 | bytes 36700160 | tf_op jit(solution)/shard_map/dot_general | solution.py:24
  28.8 0.0 reduce-scatter.2.cloned.1.call-update
  28.8 421.2 %reduce-scatter.2.cloned.1.call-done = f32[320,2560]{1,0:T(8,128)} async-done(((f32[2560,2560]{1,0:T(8,128)}), f32[320,2560]{1,0:T(8,128)}) %reduce-scatter.2.cloned.1.call-update) | async-done | bytes 3276816 | tf_op jit(solution)/shard_map/reduce_scatter | solution.py:23
  450.0 0.0 copy-start
  450.0 3.5 slice_select_fusion
  453.5 1.5 collective-permute-start
  454.9 36.5 %collective-permute-done = f32[320,1280]{1,0:T(8,128)} collective-permute-done((f32[320,1280]{1,0:T(8,128)}, f32[320,1280]{1,0:T(8,128)}, u32[]{:S(2)}, u32[]{:S(2)}) %collective-permute-start) | collective-permute-done | bytes 1638432 | tf_op jit(solution)/shard_map/ppermute | solution.py:10
  491.4 0.0 copy-done
  491.4 4.3 multiply_reduce_fusion.2
  495.7 2.0 pad_maximum_fusion
  497.7 0.1 broadcast_multiply_fusion.1
  497.7 39.3 %psum.14 = f32[3,4]{1,0:T(4,128)S(1)} all-reduce(f32[3,4]{1,0:T(4,128)S(1)} %broadcast_multiply_fusion.1), channel_id=1, replica_groups=mesh['node'=4,'fsdp'=8] {'node','fsdp'}, use_global_device_ids=true, to_apply=%region_4.5 | all-reduce | flops 12 | bytes 96 | tf_op jit(solution)/shard_map/psum | solution.py:17
  537.0 0.1 multiply_reduce_fusion.7
  537.1 0.6 fusion.1
  540.2 2.1 multiply_add_fusion
  542.4 0.1 slice_select_fusion.2
  542.4 0.1 collective-permute-start.1
  542.5 2.3 collective-permute-done.1
  544.8 1.1 multiply_reduce_fusion.5
  545.9 2.0 pad_maximum_fusion.1
  547.9 0.1 broadcast_multiply_fusion
  548.0 39.8 %psum.15 = f32[3,4]{1,0:T(4,128)S(1)} all-reduce(f32[3,4]{1,0:T(4,128)S(1)} %broadcast_multiply_fusion), channel_id=1, replica_groups=mesh['node'=4,'fsdp'=8] {'node','fsdp'}, use_global_device_ids=true, to_apply=%region_9.10 | all-reduce | flops 12 | bytes 96 | tf_op jit(solution)/shard_map/psum | solution.py:17
  587.8 0.1 multiply_reduce_fusion.6
  587.9 0.7 fusion
  591.2 1.0 multiply_add_fusion.1
  (2 shorter events, 0.0 us)
Async XLA Ops:
  6.5 443.5 %reduce-scatter.2.cloned.1.call-start = ((), (), s32[]{:S(2)}) async-start(), calls=%async_computation.1 | async-start | bytes 29491200 | tf_op jit(solution)/shard_map/reduce_scatter | solution.py:23
  450.0 41.4 %copy-start = (f32[320,2560]{1,0:T(8,128)S(1)}, f32[320,2560]{1,0:T(8,128)}, u32[]{:S(2)}) copy-start(f32[320,2560]{1,0:T(8,128)} %reduce-scatter.2.cloned.1.call-done) | copy-start | bytes 9830404
  453.5 37.9 %collective-permute-start = (f32[320,1280]{1,0:T(8,128)}, f32[320,1280]{1,0:T(8,128)}, u32[]{:S(2)}, u32[]{:S(2)}) collective-permute-start(f32[320,1280]{1,0:T(8,128)} %slice_select_fusion), channel_id=1, source_target_pairs={{0,16},{8,24},{16,0},{24,8},{1,17},{9,25},{17,1},{25,9},{2,18},{10... | collective-permute-start | bytes 4915208 | tf_op jit(solution)/shard_map/ppermute | solution.py:10
  542.4 2.4 collective-permute-start.1
Sparse Core Ops, SparseCore 0:
  28.9 421.0 reduce-scatter.1
where the time goes:
time: 600 us; the launch traced here: 599 us
  waiting for transfers between devices  460 us (77%)
  blocking collectives  79.1 us (13%)
  matrix products  22.2 us (4%)
  between operations  18.6 us (3%)
  other arithmetic  16.3 us (3%)
    reduce_scatter x1, waiting for transfers between devices, local(): lax.psum_scatter(lax.dot_general(activations, grad_out, (((0,), (0,)), ((...  421 us
    psum x2, blocking collectives, group_totals(): totals = lax.psum(spread, ('node', 'fsdp'))  79.1 us
    ppermute x2, waiting for transfers between devices, partner(): lax.ppermute(array, axis, [(i, i ^ 1 << distance) for i in range(lax.axis...  38.8 us
    dot_general x1, matrix products, local(): lax.dot_general(activations, grad_out, (((0,), (0,)), ((), ())), preferre...  22.2 us
  transfers between devices with their start and end apart: 3, of which 3 were waited for; matrix products, arithmetic and copies ran while one was open for 0% of the time, Pallas kernels for 0%

commit v1 on v0

v1 whole, which is shorter than its diff:
```python
import functools

import jax
import jax.numpy as jnp
from jax import lax
from jax.experimental import pallas as pl
from jax.experimental.pallas import tpu as pltpu
from jax.sharding import PartitionSpec as P

EPS = 1e-06
MESH = pl.DeviceIdType.MESH
TOP = 2.0**14
Z_SIZE = 4


def ring_place(position, count):
    x_size = count // Z_SIZE
    inner = x_size - 1
    past = (position + count - Z_SIZE) // count
    rest = (position - Z_SIZE + count) % count
    line = rest // inner
    step = rest % inner
    odd = line % 2
    x = (1 - odd) * (1 + step) + odd * (x_size - 1 - step)
    z = Z_SIZE - 1 - line
    return past * (z * x_size + x) + (1 - past) * position * x_size


def ring_position(index, count):
    x_size = count // Z_SIZE
    inner = x_size - 1
    z = index // x_size
    x = index % x_size
    past = (x + inner) // x_size
    line = Z_SIZE - 1 - z
    odd = line % 2
    step = (1 - odd) * (x - 1) + odd * (x_size - 1 - x)
    return past * (Z_SIZE + line * inner + step) + (1 - past) * z


def encode(value, top):
    x = value * (TOP / top)
    square = x * x
    fourth = square * square
    eighth = fourth * fourth
    return jnp.where(x < 0, -eighth, eighth).astype(jnp.bfloat16)


def decode(code, top):
    y = code.astype(jnp.float32)
    root = lax.rsqrt(lax.rsqrt(jnp.maximum(jnp.abs(y), 1e-37)))
    value = root * lax.rsqrt(root) * (top * (1.0 / TOP))
    return jnp.where(y < 0, -value, value)


def kernel(
    nodes, count, at_ref, g_ref, out_ref,
    sent, came, sent_top, came_top, acc, own, gathered, sums_mine, sums_came,
    send_sem, recv_sem, top_send, top_recv, swap_send, swap_recv, sum_send, sum_recv,
):
    node = lax.axis_index("node")
    place = lax.axis_index("fsdp")
    rows, cols = acc.shape
    me = ring_position(place, count)
    right = ring_place((me + 1) % count, count)
    left = ring_place((me + count - 1) % count, count)
    half = count // 2

    barrier = pltpu.get_barrier_semaphore()
    for k in range(1, count):
        pl.semaphore_signal(barrier, inc=1, device_id=(node, (place + k) % count), device_id_type=MESH)
    for k in range(1, nodes):
        pl.semaphore_signal(barrier, inc=1, device_id=((node + k) % nodes, place), device_id_type=MESH)
    pl.semaphore_wait(barrier, count + nodes - 2)

    def product(owner, block):
        if g_ref.ndim == 3:
            g = g_ref[block]
        else:
            g = g_ref[:, pl.ds(pl.multiple_of(block * cols, cols), cols)]
        acc[...] = jnp.dot(at_ref[owner], g, preferred_element_type=jnp.float32)

    def copies(side, block, step):
        target = (node, right if side == 0 else left)
        data = pltpu.make_async_remote_copy(
            src_ref=sent.at[side, block, step], dst_ref=came.at[side, block, step],
            send_sem=send_sem.at[side, block, step], recv_sem=recv_sem.at[side, block, step],
            device_id=target, device_id_type=MESH)
        top = pltpu.make_async_remote_copy(
            src_ref=sent_top.at[side, block, step], dst_ref=came_top.at[side, block, step],
            send_sem=top_send.at[side, block, step], recv_sem=top_recv.at[side, block, step],
            device_id=target, device_id_type=MESH)
        return data, top

    def add_arrived(side, block, step):
        data, top = copies(side, block, step)
        top.wait_recv()
        data.wait_recv()
        largest = came_top[side, block, step][0:1, 0:1].astype(jnp.float32)
        acc[...] += decode(came[side, block, step], largest)

    def hops(side, parity):
        return half if side == parity else count - 1 - half

    def send_on(side, parity, block, step):
        distance = hops(side, parity) - step
        far = (me + distance) % count if side == 0 else (me + count - distance) % count
        product(ring_place(far, count), block)

        @pl.when(step > 0)
        def _():
            add_arrived(side, block, step - 1)

        largest = jnp.maximum(jnp.max(jnp.abs(acc[...]), axis=(0, 1), keepdims=True), 1e-30)
        tile = jnp.broadcast_to(largest, (16, 128)).astype(jnp.bfloat16)
        sent_top[side, block, step] = tile
        sent[side, block, step] = encode(acc[...], tile[0:1, 0:1].astype(jnp.float32))
        data, top = copies(side, block, step)
        top.start()
        data.start()

    def swap(block):
        return pltpu.make_async_remote_copy(
            src_ref=own.at[block], dst_ref=gathered.at[node],
            send_sem=swap_send.at[block], recv_sem=swap_recv.at[node],
            device_id=(block, place), device_id_type=MESH)

    def finish(parity, block):
        product(place, block)
        for side in range(2):
            add_arrived(side, block, hops(side, parity) - 1)

        @pl.when(block != node)
        def _():
            own[block] = acc[...]
            swap(block).start()

        @pl.when(block == node)
        def _():
            gathered[block] = acc[...]

    @pl.loop(0, nodes // 2)
    def _(pair):
        @pl.loop(0, half)
        def _(step):
            for parity in range(2):
                for side in range(2):
                    if side == parity:
                        send_on(side, parity, 2 * pair + parity, step)
                    else:
                        pl.when(step < half - 1)(
                            functools.partial(send_on, side, parity, 2 * pair + parity, step))

            @pl.when((step == 0) & (pair > 0))
            def _():
                for parity in range(2):
                    finish(parity, 2 * pair - 2 + parity)

    for parity in range(2):
        finish(parity, nodes - 2 + parity)

    @pl.loop(1, nodes)
    def _(k):
        other = (node + k) % nodes
        pltpu.make_async_remote_copy(
            src_ref=own.at[other], dst_ref=gathered.at[other],
            send_sem=swap_send.at[other], recv_sem=swap_recv.at[other],
            device_id=(other, place), device_id_type=MESH).wait_recv()

    def exchange(level, stage, size):
        def copy(k):
            far = (node, (place + k) % count) if stage == 0 else ((node + k) % nodes, place)
            return pltpu.make_async_remote_copy(
                src_ref=sums_mine.at[level, stage], dst_ref=sums_came.at[level, stage, k],
                send_sem=sum_send.at[level, stage, k], recv_sem=sum_recv.at[level, stage, k],
                device_id=far, device_id_type=MESH)

        for k in range(1, size):
            copy(k).start()
        total = sums_mine[level, stage]
        for k in range(1, size):
            copy(k).wait_recv()
            total = total + sums_came[level, stage, k]
        for k in range(1, size):
            copy(k).wait_send()
        return total

    def whole_sum(value):
        return jnp.sum(jnp.sum(value, axis=0, keepdims=True), axis=1, keepdims=True)

    levels = nodes.bit_length() - 1
    left_over = nodes
    for level in range(levels):
        left_over //= 2
        tile = jnp.zeros(sums_mine.shape[2:], jnp.float32)
        line = lax.broadcasted_iota(jnp.int32, tile.shape, 0)
        for j in range(left_over):
            first = gathered[j]
            second = gathered[j + left_over]
            for i, term in enumerate((first * second, first * first, second * second)):
                tile = jnp.where(line == 3 * j + i, whole_sum(term), tile)
        sums_mine[level, 0] = tile
        sums_mine[level, 1] = exchange(level, 0, count)
        total = exchange(level, 1, nodes)
        for j in range(left_over):
            inner = total[3 * j : 3 * j + 1, 0:1]
            first_sq = total[3 * j + 1 : 3 * j + 2, 0:1]
            second_sq = total[3 * j + 2 : 3 * j + 3, 0:1]
            coef_first = 1.0 - inner / (2.0 * (first_sq + EPS))
            coef_second = 1.0 - inner / (2.0 * (second_sq + EPS))
            mixed = coef_first * gathered[j] + coef_second * gathered[j + left_over]
            if left_over == 1:
                out_ref[...] = mixed
            else:
                gathered[j] = mixed

    @pl.loop(1, nodes)
    def _(k):
        swap((node + k) % nodes).wait_send()

    @pl.loop(0, nodes // 2)
    def _(pair):
        for parity in range(2):
            for side in range(2):
                @pl.loop(0, hops(side, parity))
                def _(step):
                    data, top = copies(side, 2 * pair + parity, step)
                    top.wait_send()
                    data.wait_send()


def solution(mesh):
    nodes, count = mesh.shape["node"], mesh.shape["fsdp"]

    def local(activations, grad_out):
        tokens, features = activations.shape
        columns = grad_out.shape[1]
        rows, cols = features // count, columns // nodes
        half = count // 2
        levels = nodes.bit_length() - 1
        turned = activations.T.reshape(count, rows, tokens)
        if cols % 128:
            grad_out = grad_out.reshape(tokens, nodes, cols).transpose(1, 0, 2)
        lines = -(-3 * nodes // 2 // 8) * 8
        hop = (2, nodes, half)
        dma = pltpu.SemaphoreType.DMA
        return pl.pallas_call(
            functools.partial(kernel, nodes, count),
            out_shape=jax.ShapeDtypeStruct((rows, cols), jnp.float32),
            in_specs=[pl.BlockSpec(memory_space=pltpu.VMEM)] * 2,
            out_specs=pl.BlockSpec(memory_space=pltpu.VMEM),
            scratch_shapes=[
                pltpu.VMEM(hop + (rows, cols), jnp.bfloat16),
                pltpu.VMEM(hop + (rows, cols), jnp.bfloat16),
                pltpu.VMEM(hop + (16, 128), jnp.bfloat16),
                pltpu.VMEM(hop + (16, 128), jnp.bfloat16),
                pltpu.VMEM((rows, cols), jnp.float32),
                pltpu.VMEM((nodes, rows, cols), jnp.float32),
                pltpu.VMEM((nodes, rows, cols), jnp.float32),
                pltpu.VMEM((levels, 2, lines, 128), jnp.float32),
                pltpu.VMEM((levels, 2, max(nodes, count), lines, 128), jnp.float32),
                dma(hop), dma(hop), dma(hop), dma(hop),
                dma((nodes,)), dma((nodes,)),
                dma((levels, 2, max(nodes, count))), dma((levels, 2, max(nodes, count))),
            ],
            compiler_params=pltpu.CompilerParams(
                collective_id=0, has_side_effects=True, vmem_limit_bytes=60 * 2**20),
        )(turned, grad_out)

    in_specs = (P(("node", "fsdp"), None), P(("node", "fsdp"), None))
    return jax.shard_map(local, mesh=mesh, in_specs=in_specs, out_specs=P("fsdp", "node"), check_vma=False)
```

time: 600 us -> 199 us (0.33)
  waiting for transfers between devices: 460 us -> 0 us
  Pallas kernels: 0 us -> 188 us
  blocking collectives: 79.1 us -> 0 us
  matrix products: 22.2 us -> 0 us
  between operations: 18.6 us -> 0.01 us
  other arithmetic: 16.3 us -> 0 us
  local copies, waits for them, and re-layouts: 1.29 us -> 10 us
    reduce_scatter x1 -> x0, waiting for transfers between devices: 421 us -> none  [local(): lax.psum_scatter(lax.dot_general(activations, grad_out, (((0,), (0,)), ((...]
    pallas_call x0 -> x1, Pallas kernels: none -> 188 us  [local(): pl.pallas_call(functools.partial(kernel, nodes, count), out_shape=jax.Sha...]
    psum x2 -> x0, blocking collectives: 79.1 us -> none  [group_totals(): totals = lax.psum(spread, ('node', 'fsdp'))]
    ppermute x2 -> x0, waiting for transfers between devices: 38.8 us -> none  [partner(): lax.ppermute(array, axis, [(i, i ^ 1 << distance) for i in range(lax.axis...]
    dot_general x1 -> x0, matrix products: 22.2 us -> none  [local(): lax.dot_general(activations, grad_out, (((0,), (0,)), ((), ())), preferre...]
    transpose x0 -> x1, local copies, waits for them, and re-layouts: none -> 7.96 us  [local(): turned = activations.T.reshape(count, rows, tokens)]
  transfers between devices with their start and end apart: 3 -> 0, of which waited for: 3 -> 0; matrix products, arithmetic and copies ran while one was open for 0% -> 0% of each run, Pallas kernels for 0% -> 0%
where the time goes in v1:
time: 199 us; the launch traced here: 198 us
  Pallas kernels  188 us (94%)
  local copies, waits for them, and re-layouts  10 us (5%)
    pallas_call x1, Pallas kernels, local(): pl.pallas_call(functools.partial(kernel, nodes, count), out_shape=jax.Sha...  188 us
    transpose x1, local copies, waits for them, and re-layouts, local(): turned = activations.T.reshape(count, rows, tokens)  7.96 us

profile of v1, /device:TPU:0, one launch (start us, length us, event | category | flops | bytes accessed | tf_op | source)
XLA Modules:
  0.0 198.4 jit_solution(9366122368321095489)
XLA Ops:
  0.0 8.0 %copy.3 = bf16[2560,1024]{1,0:T(8,128)(2,1)} copy(bf16[2560,1024]{0,1:T(8,128)(2,1)} %bitcast.3) | data formatting | bytes 10485760 | tf_op jit(solution)/shard_map/transpose | solution.py:241
  8.0 188.4 %shard_map.28 = f32[320,640]{1,0:T(8,128)} custom-call(bf16[8,320,1024]{2,1,0:T(8,128)(2,1)} %bitcast.2, bf16[1024,2560]{1,0:T(8,128)(2,1)} %g_ref.1), custom_call_target="tpu_custom_call" | custom-call | tf_op jit(solution)/shard_map/pallas_call | solution.py:247
  196.3 2.1 %copy.5 = f32[320,640]{1,0:T(8,128)} copy(f32[320,640]{1,0:T(8,128)} %shard_map.28) | data formatting | bytes 1638400

commit v2 on v1

--- a/solution.py
+++ b/solution.py
@@ -11,6 +11,7 @@
 MESH = pl.DeviceIdType.MESH
 TOP = 2.0**14
 Z_SIZE = 4
+CHUNK = 16
 
 
 def ring_place(position, count):
@@ -38,8 +39,8 @@
     return past * (Z_SIZE + line * inner + step) + (1 - past) * z
 
 
-def encode(value, top):
-    x = value * (TOP / top)
+def encode(value, scale):
+    x = value * scale
     square = x * x
     fourth = square * square
     eighth = fourth * fourth
@@ -55,7 +56,7 @@
 
 def kernel(
     nodes, count, at_ref, g_ref, out_ref,
-    sent, came, sent_top, came_top, acc, own, gathered, sums_mine, sums_came,
+    sent, came, sent_top, came_top, acc, peaks, own, gathered, sums_mine, sums_came,
     send_sem, recv_sem, top_send, top_recv, swap_send, swap_recv, sum_send, sum_recv,
 ):
     node = lax.axis_index("node")
@@ -92,12 +93,17 @@
             device_id=target, device_id_type=MESH)
         return data, top
 
-    def add_arrived(side, block, step):
+    def by_chunk(body, start=None):
+        def step(i, carry):
+            return body(pl.ds(pl.multiple_of(i * CHUNK, CHUNK), CHUNK), carry)
+
+        return lax.fori_loop(0, rows // CHUNK, step, start, unroll=2)
+
+    def arrived(side, block, step):
         data, top = copies(side, block, step)
         top.wait_recv()
         data.wait_recv()
-        largest = came_top[side, block, step][0:1, 0:1].astype(jnp.float32)
-        acc[...] += decode(came[side, block, step], largest)
+        return came_top[side, block, step][0:1, 0:1].astype(jnp.float32)
 
     def hops(side, parity):
         return half if side == parity else count - 1 - half
@@ -109,12 +115,29 @@
 
         @pl.when(step > 0)
         def _():
-            add_arrived(side, block, step - 1)
-
-        largest = jnp.maximum(jnp.max(jnp.abs(acc[...]), axis=(0, 1), keepdims=True), 1e-30)
+            top = arrived(side, block, step - 1)
+
+            def add(part, peak):
+                value = acc[part, :] + decode(came[side, block, step - 1, part, :], top)
+                acc[part, :] = value
+                return jnp.maximum(peak, jnp.abs(value))
+
+            peaks[...] = by_chunk(add, jnp.zeros(peaks.shape, jnp.float32))
+
+        @pl.when(step == 0)
+        def _():
+            peaks[...] = by_chunk(
+                lambda part, peak: jnp.maximum(peak, jnp.abs(acc[part, :])), jnp.zeros(peaks.shape, jnp.float32))
+
+        largest = jnp.maximum(jnp.max(peaks[...], axis=(0, 1), keepdims=True), 1e-30)
         tile = jnp.broadcast_to(largest, (16, 128)).astype(jnp.bfloat16)
         sent_top[side, block, step] = tile
-        sent[side, block, step] = encode(acc[...], tile[0:1, 0:1].astype(jnp.float32))
+        scale = TOP / tile[0:1, 0:1].astype(jnp.float32)
+
+        def code(part, carry):
+            sent[side, block, step, part, :] = encode(acc[part, :], scale)
+
+        by_chunk(code)
         data, top = copies(side, block, step)
         top.start()
         data.start()
@@ -127,20 +150,37 @@
 
     def finish(parity, block):
         product(place, block)
-        for side in range(2):
-            add_arrived(side, block, hops(side, parity) - 1)
+        steps = [hops(side, parity) - 1 for side in range(2)]
+        tops = [arrived(side, block, steps[side]) for side in range(2)]
+
+        def total(part):
+            value = acc[part, :]
+            for side in range(2):
+                value = value + decode(came[side, block, steps[side], part, :], tops[side])
+            return value
 
         @pl.when(block != node)
         def _():
-            own[block] = acc[...]
+            def store(part, carry):
+                own[block, part, :] = total(part)
+
+            by_chunk(store)
             swap(block).start()
 
         @pl.when(block == node)
         def _():
-            gathered[block] = acc[...]
+            def store(part, carry):
+                gathered[block, part, :] = total(part)
+
+            by_chunk(store)
+
+    def pair_at(turn):
+        return (node // 2 + 1 + turn) % (nodes // 2)
 
     @pl.loop(0, nodes // 2)
-    def _(pair):
+    def _(turn):
+        pair = pair_at(turn)
+
         @pl.loop(0, half)
         def _(step):
             for parity in range(2):
@@ -151,13 +191,13 @@
                         pl.when(step < half - 1)(
                             functools.partial(send_on, side, parity, 2 * pair + parity, step))
 
-            @pl.when((step == 0) & (pair > 0))
+            @pl.when((step == 0) & (turn > 0))
             def _():
                 for parity in range(2):
-                    finish(parity, 2 * pair - 2 + parity)
+                    finish(parity, 2 * pair_at(turn - 1) + parity)
 
     for parity in range(2):
-        finish(parity, nodes - 2 + parity)
+        finish(parity, 2 * pair_at(nodes // 2 - 1) + parity)
 
     @pl.loop(1, nodes)
     def _(k):
@@ -195,9 +235,12 @@
         tile = jnp.zeros(sums_mine.shape[2:], jnp.float32)
         line = lax.broadcasted_iota(jnp.int32, tile.shape, 0)
         for j in range(left_over):
-            first = gathered[j]
-            second = gathered[j + left_over]
-            for i, term in enumerate((first * second, first * first, second * second)):
+            def add(part, sums):
+                first = gathered[j, part, :]
+                second = gathered[j + left_over, part, :]
+                return sums[0] + first * second, sums[1] + first * first, sums[2] + second * second
+
+            for i, term in enumerate(by_chunk(add, (jnp.zeros(peaks.shape, jnp.float32),) * 3)):
                 tile = jnp.where(line == 3 * j + i, whole_sum(term), tile)
         sums_mine[level, 0] = tile
         sums_mine[level, 1] = exchange(level, 0, count)
@@ -208,11 +251,15 @@
             second_sq = total[3 * j + 2 : 3 * j + 3, 0:1]
             coef_first = 1.0 - inner / (2.0 * (first_sq + EPS))
             coef_second = 1.0 - inner / (2.0 * (second_sq + EPS))
-            mixed = coef_first * gathered[j] + coef_second * gathered[j + left_over]
-            if left_over == 1:
-                out_ref[...] = mixed
-            else:
-                gathered[j] = mixed
+
+            def mix(part, carry):
+                mixed = coef_first * gathered[j, part, :] + coef_second * gathered[j + left_over, part, :]
+                if left_over == 1:
+                    out_ref[part, :] = mixed
+                else:
+                    gathered[j, part, :] = mixed
+
+            by_chunk(mix)
 
     @pl.loop(1, nodes)
     def _(k):
@@ -255,6 +302,7 @@
                 pltpu.VMEM(hop + (16, 128), jnp.bfloat16),
                 pltpu.VMEM(hop + (16, 128), jnp.bfloat16),
                 pltpu.VMEM((rows, cols), jnp.float32),
+                pltpu.VMEM((CHUNK, cols), jnp.float32),
                 pltpu.VMEM((nodes, rows, cols), jnp.float32),
                 pltpu.VMEM((nodes, rows, cols), jnp.float32),
                 pltpu.VMEM((levels, 2, lines, 128), jnp.float32),

time: 199 us -> 173 us (0.87)
  Pallas kernels: 188 us -> 163 us
    pallas_call x1, Pallas kernels: 188 us -> 163 us  [local(): pl.pallas_call(functools.partial(kernel, nodes, count), out_shape=jax.Sha...]
where the time goes in v2:
time: 173 us
  Pallas kernels  163 us (94%)
  local copies, waits for them, and re-layouts  10 us (6%)
    pallas_call x1, Pallas kernels, local(): pl.pallas_call(functools.partial(kernel, nodes, count), out_shape=jax.Sha...  163 us
    transpose x1, local copies, waits for them, and re-layouts, local(): turned = activations.T.reshape(count, rows, tokens)  7.96 us

profile of v2, /device:TPU:0, one launch (start us, length us, event | category | flops | bytes accessed | tf_op | source)
XLA Modules:
  0.0 172.7 jit_solution(17445810762122735373)
XLA Ops:
  0.0 8.0 %copy.3 = bf16[2560,1024]{1,0:T(8,128)(2,1)} copy(bf16[2560,1024]{0,1:T(8,128)(2,1)} %bitcast.3) | data formatting | bytes 10485760 | tf_op jit(solution)/shard_map/transpose | solution.py:288
  8.0 162.6 %shard_map.28 = f32[320,640]{1,0:T(8,128)} custom-call(bf16[8,320,1024]{2,1,0:T(8,128)(2,1)} %bitcast.2, bf16[1024,2560]{1,0:T(8,128)(2,1)} %g_ref.1), custom_call_target="tpu_custom_call" | custom-call | tf_op jit(solution)/shard_map/pallas_call | solution.py:294
  170.6 2.1 %copy.5 = f32[320,640]{1,0:T(8,128)} copy(f32[320,640]{1,0:T(8,128)} %shard_map.28) | data formatting | bytes 1638400

commit v3 on v2

--- a/solution.py
+++ b/solution.py
@@ -55,9 +55,9 @@
 
 
 def kernel(
-    nodes, count, at_ref, g_ref, out_ref,
-    sent, came, sent_top, came_top, acc, peaks, own, gathered, sums_mine, sums_came,
-    send_sem, recv_sem, top_send, top_recv, swap_send, swap_recv, sum_send, sum_recv,
+    nodes, count, a_ref, g_hbm, out_ref,
+    raw, at_ref, g_ref, sent, came, sent_top, came_top, acc, peaks, own, gathered, sums_mine, sums_came,
+    a_sem, g_sem, send_sem, recv_sem, top_send, top_recv, swap_send, swap_recv, sum_send, sum_recv,
 ):
     node = lax.axis_index("node")
     place = lax.axis_index("fsdp")
@@ -67,19 +67,55 @@
     left = ring_place((me + count - 1) % count, count)
     half = count // 2
 
+    x_size = count // Z_SIZE
+    width = raw.shape[1] // Z_SIZE
+    far_group = ring_place((me + half) % count, count) // x_size
+
+    def pair_at(turn):
+        return (node // 2 + 1 + turn) % (nodes // 2)
+
+    def g_view(ref, block):
+        if ref.ndim == 3:
+            return ref.at[block]
+        return ref.at[:, pl.ds(pl.multiple_of(block * cols, cols), cols)]
+
+    def a_load(group):
+        part = pl.ds(pl.multiple_of(group * width, 128), width)
+        return pltpu.make_async_copy(a_ref.at[:, part], raw.at[:, part], a_sem.at[group])
+
+    def g_load(block):
+        return pltpu.make_async_copy(g_view(g_hbm, block), g_view(g_ref, block), g_sem.at[block])
+
     barrier = pltpu.get_barrier_semaphore()
     for k in range(1, count):
         pl.semaphore_signal(barrier, inc=1, device_id=(node, (place + k) % count), device_id_type=MESH)
     for k in range(1, nodes):
         pl.semaphore_signal(barrier, inc=1, device_id=((node + k) % nodes, place), device_id_type=MESH)
+    a_load(far_group).start()
+    for parity in range(2):
+        g_load(2 * pair_at(0) + parity).start()
+    for k in range(1, Z_SIZE):
+        a_load((far_group + k) % Z_SIZE).start()
+
+    @pl.loop(1, nodes // 2)
+    def _(turn):
+        for parity in range(2):
+            g_load(2 * pair_at(turn) + parity).start()
+
+    def transpose_group(group):
+        a_load(group).wait()
+
+        @pl.loop(0, width // 128)
+        def _(i):
+            part = pl.ds(pl.multiple_of(group * width + i * 128, 128), 128)
+            at_ref[part, :] = raw[:, part].T
+
+    transpose_group(far_group)
     pl.semaphore_wait(barrier, count + nodes - 2)
 
     def product(owner, block):
-        if g_ref.ndim == 3:
-            g = g_ref[block]
-        else:
-            g = g_ref[:, pl.ds(pl.multiple_of(block * cols, cols), cols)]
-        acc[...] = jnp.dot(at_ref[owner], g, preferred_element_type=jnp.float32)
+        mine = at_ref[pl.ds(pl.multiple_of(owner * rows, 16), rows), :]
+        acc[...] = jnp.dot(mine, g_view(g_ref, block)[...], preferred_element_type=jnp.float32)
 
     def copies(side, block, step):
         target = (node, right if side == 0 else left)
@@ -148,16 +184,20 @@
             send_sem=swap_send.at[block], recv_sem=swap_recv.at[node],
             device_id=(block, place), device_id_type=MESH)
 
+    def prepare(parity, block):
+        product(place, block)
+        top = arrived(1 - parity, block, half - 2)
+
+        def add(part, carry):
+            own[block, part, :] = acc[part, :] + decode(came[1 - parity, block, half - 2, part, :], top)
+
+        by_chunk(add)
+
     def finish(parity, block):
-        product(place, block)
-        steps = [hops(side, parity) - 1 for side in range(2)]
-        tops = [arrived(side, block, steps[side]) for side in range(2)]
+        top = arrived(parity, block, half - 1)
 
         def total(part):
-            value = acc[part, :]
-            for side in range(2):
-                value = value + decode(came[side, block, steps[side], part, :], tops[side])
-            return value
+            return own[block, part, :] + decode(came[parity, block, half - 1, part, :], top)
 
         @pl.when(block != node)
         def _():
@@ -174,30 +214,38 @@
 
             by_chunk(store)
 
-    def pair_at(turn):
-        return (node // 2 + 1 + turn) % (nodes // 2)
+    def finish_pair(turn):
+        for parity in range(2):
+            prepare(parity, 2 * pair_at(turn) + parity)
+        for parity in range(2):
+            finish(parity, 2 * pair_at(turn) + parity)
 
     @pl.loop(0, nodes // 2)
     def _(turn):
         pair = pair_at(turn)
+        for parity in range(2):
+            g_load(2 * pair + parity).wait()
 
         @pl.loop(0, half)
         def _(step):
-            for parity in range(2):
+            for side in range(2):
+                send_on(side, side, 2 * pair + side, step)
+
+            @pl.when((turn == 0) & (step == 0))
+            def _():
+                for k in range(1, Z_SIZE):
+                    transpose_group((far_group + k) % Z_SIZE)
+
+            @pl.when(step < half - 1)
+            def _():
                 for side in range(2):
-                    if side == parity:
-                        send_on(side, parity, 2 * pair + parity, step)
-                    else:
-                        pl.when(step < half - 1)(
-                            functools.partial(send_on, side, parity, 2 * pair + parity, step))
+                    send_on(side, 1 - side, 2 * pair + 1 - side, step)
 
             @pl.when((step == 0) & (turn > 0))
             def _():
-                for parity in range(2):
-                    finish(parity, 2 * pair_at(turn - 1) + parity)
-
-    for parity in range(2):
-        finish(parity, 2 * pair_at(nodes // 2 - 1) + parity)
+                finish_pair(turn - 1)
+
+    finish_pair(nodes // 2 - 1)
 
     @pl.loop(1, nodes)
     def _(k):
@@ -285,7 +333,6 @@
         rows, cols = features // count, columns // nodes
         half = count // 2
         levels = nodes.bit_length() - 1
-        turned = activations.T.reshape(count, rows, tokens)
         if cols % 128:
             grad_out = grad_out.reshape(tokens, nodes, cols).transpose(1, 0, 2)
         lines = -(-3 * nodes // 2 // 8) * 8
@@ -294,9 +341,12 @@
         return pl.pallas_call(
             functools.partial(kernel, nodes, count),
             out_shape=jax.ShapeDtypeStruct((rows, cols), jnp.float32),
-            in_specs=[pl.BlockSpec(memory_space=pltpu.VMEM)] * 2,
+            in_specs=[pl.BlockSpec(memory_space=pl.ANY)] * 2,
             out_specs=pl.BlockSpec(memory_space=pltpu.VMEM),
             scratch_shapes=[
+                pltpu.VMEM((tokens, features), jnp.bfloat16),
+                pltpu.VMEM((features, tokens), jnp.bfloat16),
+                pltpu.VMEM(grad_out.shape, jnp.bfloat16),
                 pltpu.VMEM(hop + (rows, cols), jnp.bfloat16),
                 pltpu.VMEM(hop + (rows, cols), jnp.bfloat16),
                 pltpu.VMEM(hop + (16, 128), jnp.bfloat16),
@@ -307,13 +357,14 @@
                 pltpu.VMEM((nodes, rows, cols), jnp.float32),
                 pltpu.VMEM((levels, 2, lines, 128), jnp.float32),
                 pltpu.VMEM((levels, 2, max(nodes, count), lines, 128), jnp.float32),
+                dma((Z_SIZE,)), dma((nodes,)),
                 dma(hop), dma(hop), dma(hop), dma(hop),
                 dma((nodes,)), dma((nodes,)),
                 dma((levels, 2, max(nodes, count))), dma((levels, 2, max(nodes, count))),
             ],
             compiler_params=pltpu.CompilerParams(
                 collective_id=0, has_side_effects=True, vmem_limit_bytes=60 * 2**20),
-        )(turned, grad_out)
+        )(activations, grad_out)
 
     in_specs = (P(("node", "fsdp"), None), P(("node", "fsdp"), None))
     return jax.shard_map(local, mesh=mesh, in_specs=in_specs, out_specs=P("fsdp", "node"), check_vma=False)

time: 173 us -> 156 us (0.902)
  Pallas kernels: 163 us -> 154 us
  local copies, waits for them, and re-layouts: 10 us -> 2.09 us
    pallas_call x1, Pallas kernels: 163 us -> 154 us  [local(): pl.pallas_call(functools.partial(kernel, nodes, count), out_shape=jax.Sha...]
    transpose x1 -> x0, local copies, waits for them, and re-layouts: 7.96 us -> none  [local(): turned = activations.T.reshape(count, rows, tokens)]
where the time goes in v3:
time: 156 us
  Pallas kernels  154 us (99%)
  local copies, waits for them, and re-layouts  2.09 us (1%)
    pallas_call x1, Pallas kernels, local(): pl.pallas_call(functools.partial(kernel, nodes, count), out_shape=jax.Sha...  154 us

profile of v3, /device:TPU:0, one launch (start us, length us, event | category | flops | bytes accessed | tf_op | source)
XLA Modules:
  0.0 156.3 jit_solution(2707353234611808110)
XLA Ops:
  0.0 154.2 %shard_map.28 = f32[320,640]{1,0:T(8,128)} custom-call(bf16[1024,2560]{1,0:T(8,128)(2,1)} %a_ref.1, bf16[1024,2560]{1,0:T(8,128)(2,1)} %g_hbm.1), custom_call_target="tpu_custom_call" | custom-call | tf_op jit(solution)/shard_map/pallas_call | solution.py:341
  154.2 2.1 %copy.4 = f32[320,640]{1,0:T(8,128)} copy(f32[320,640]{1,0:T(8,128)} %shard_map.28) | data formatting | bytes 1638400

commit v4 on v3

--- a/solution.py
+++ b/solution.py
@@ -118,7 +118,7 @@
         acc[...] = jnp.dot(mine, g_view(g_ref, block)[...], preferred_element_type=jnp.float32)
 
     def copies(side, block, step):
-        target = (node, right if side == 0 else left)
+        target = (node, right * (1 - side) + left * side)
         data = pltpu.make_async_remote_copy(
             src_ref=sent.at[side, block, step], dst_ref=came.at[side, block, step],
             send_sem=send_sem.at[side, block, step], recv_sem=recv_sem.at[side, block, step],
@@ -217,7 +217,7 @@
     def finish_pair(turn):
         for parity in range(2):
             prepare(parity, 2 * pair_at(turn) + parity)
-        for parity in range(2):
+        for parity in (1 - node % 2, node % 2):
             finish(parity, 2 * pair_at(turn) + parity)
 
     @pl.loop(0, nodes // 2)
@@ -276,38 +276,100 @@
     def whole_sum(value):
         return jnp.sum(jnp.sum(value, axis=0, keepdims=True), axis=1, keepdims=True)
 
-    levels = nodes.bit_length() - 1
-    left_over = nodes
-    for level in range(levels):
-        left_over //= 2
+    def fold(value):
+        if cols % 128:
+            return value
+        return sum(value[:, i : i + 128] for i in range(0, cols, 128))
+
+    def reduce_all(level, pairs_of, number):
+        def step(i, sums):
+            part = pl.ds(pl.multiple_of(i * 8, 8), 8)
+            return tuple(t + fold(a * b) for t, (a, b) in zip(sums, pairs_of(part)))
+
+        start = jnp.zeros((8, cols if cols % 128 else 128), jnp.float32)
+        sums = lax.fori_loop(0, rows // 8, step, (start,) * number, unroll=2)
         tile = jnp.zeros(sums_mine.shape[2:], jnp.float32)
         line = lax.broadcasted_iota(jnp.int32, tile.shape, 0)
-        for j in range(left_over):
-            def add(part, sums):
-                first = gathered[j, part, :]
-                second = gathered[j + left_over, part, :]
-                return sums[0] + first * second, sums[1] + first * first, sums[2] + second * second
-
-            for i, term in enumerate(by_chunk(add, (jnp.zeros(peaks.shape, jnp.float32),) * 3)):
-                tile = jnp.where(line == 3 * j + i, whole_sum(term), tile)
+        for i, term in enumerate(sums):
+            tile = jnp.where(line == i, whole_sum(term), tile)
         sums_mine[level, 0] = tile
         sums_mine[level, 1] = exchange(level, 0, count)
         total = exchange(level, 1, nodes)
-        for j in range(left_over):
-            inner = total[3 * j : 3 * j + 1, 0:1]
-            first_sq = total[3 * j + 1 : 3 * j + 2, 0:1]
-            second_sq = total[3 * j + 2 : 3 * j + 3, 0:1]
-            coef_first = 1.0 - inner / (2.0 * (first_sq + EPS))
-            coef_second = 1.0 - inner / (2.0 * (second_sq + EPS))
+        return [total[i : i + 1, 0:1] for i in range(number)]
+
+    def coefs(inner, first_sq, second_sq):
+        return 1.0 - inner / (2.0 * (first_sq + EPS)), 1.0 - inner / (2.0 * (second_sq + EPS))
+
+    def one_level(level, left):
+        def products(part):
+            for j in range(left):
+                first, second = gathered[j, part, :], gathered[j + left, part, :]
+                yield from ((first, second), (first, first), (second, second))
+
+        sums = reduce_all(level, products, 3 * left)
+        for j in range(left):
+            coef_first, coef_second = coefs(*sums[3 * j : 3 * j + 3])
 
             def mix(part, carry):
-                mixed = coef_first * gathered[j, part, :] + coef_second * gathered[j + left_over, part, :]
-                if left_over == 1:
+                mixed = coef_first * gathered[j, part, :] + coef_second * gathered[j + left, part, :]
+                if left == 1:
                     out_ref[part, :] = mixed
                 else:
                     gathered[j, part, :] = mixed
 
             by_chunk(mix)
+
+    def two_levels(level):
+        def products(part):
+            bases = []
+            for j in range(2):
+                first, second = gathered[j, part, :], gathered[j + 2, part, :]
+                both = first + second
+                bases.append((first, second, both))
+                yield from ((first, second), (first, first), (second, second), (both, both), (both, first - second))
+            for left in bases[0]:
+                for right in bases[1]:
+                    yield left, right
+
+        sums = reduce_all(level, products, 19)
+        pairs = []
+        for j in range(2):
+            inner, first_sq, second_sq, both_sq, cross = sums[5 * j : 5 * j + 5]
+            first, second = coefs(inner, first_sq, second_sq)
+            cancels = both_sq < 0.25 * (first_sq + second_sq)
+            mean = 0.5 * (first + second)
+            gap = 0.25 * (inner / (first_sq + EPS)) * (cross / (second_sq + EPS))
+            plain = first * (first * first_sq) + 2.0 * (first * (second * inner)) + second * (second * second_sq)
+            apart_sq = first_sq + second_sq - 2.0 * inner
+            by_sum = mean * (mean * both_sq) + 2.0 * (mean * (gap * cross)) + gap * (gap * apart_sq)
+            weights = (jnp.where(cancels, gap, first), jnp.where(cancels, -gap, second), mean)
+            pairs.append((first, second, jnp.where(cancels, by_sum, plain), cancels, weights))
+        inner = jnp.zeros((1, 1), jnp.float32)
+        for i in range(3):
+            for k in range(3):
+                term = pairs[0][4][i] * (pairs[1][4][k] * sums[10 + 3 * i + k])
+                if i == 2:
+                    term = jnp.where(pairs[0][3], term, 0.0)
+                if k == 2:
+                    term = jnp.where(pairs[1][3], term, 0.0)
+                inner = inner + term
+        low, high = coefs(inner, pairs[0][2], pairs[1][2])
+
+        def mix(part, carry):
+            below = pairs[0][0] * gathered[0, part, :] + pairs[0][1] * gathered[2, part, :]
+            above = pairs[1][0] * gathered[1, part, :] + pairs[1][1] * gathered[3, part, :]
+            out_ref[part, :] = low * below + high * above
+
+        by_chunk(mix)
+
+    level, matrices = 0, nodes
+    while matrices > 1:
+        if matrices == 4:
+            two_levels(level)
+            break
+        matrices //= 2
+        one_level(level, matrices)
+        level += 1
 
     @pl.loop(1, nodes)
     def _(k):
@@ -335,7 +397,7 @@
         levels = nodes.bit_length() - 1
         if cols % 128:
             grad_out = grad_out.reshape(tokens, nodes, cols).transpose(1, 0, 2)
-        lines = -(-3 * nodes // 2 // 8) * 8
+        lines = max(24, -(-3 * nodes // 2 // 8) * 8)
         hop = (2, nodes, half)
         dma = pltpu.SemaphoreType.DMA
         return pl.pallas_call(

time: 156 us -> 150 us (0.962)
  Pallas kernels: 154 us -> 148 us
    pallas_call x1, Pallas kernels: 154 us -> 148 us  [local(): pl.pallas_call(functools.partial(kernel, nodes, count), out_shape=jax.Sha...]
where the time goes in v4:
time: 150 us
  Pallas kernels  148 us (99%)
  local copies, waits for them, and re-layouts  2.09 us (1%)
    pallas_call x1, Pallas kernels, local(): pl.pallas_call(functools.partial(kernel, nodes, count), out_shape=jax.Sha...  148 us

profile of v4, /device:TPU:0, one launch (start us, length us, event | category | flops | bytes accessed | tf_op | source)
XLA Modules:
  0.0 149.8 jit_solution(901573896300924084)
XLA Ops:
  0.0 147.8 %shard_map.28 = f32[320,640]{1,0:T(8,128)} custom-call(bf16[1024,2560]{1,0:T(8,128)(2,1)} %a_ref.1, bf16[1024,2560]{1,0:T(8,128)(2,1)} %g_hbm.1), custom_call_target="tpu_custom_call" | custom-call | tf_op jit(solution)/shard_map/pallas_call | solution.py:403
  147.8 2.1 %copy.4 = f32[320,640]{1,0:T(8,128)} copy(f32[320,640]{1,0:T(8,128)} %shard_map.28) | data formatting | bytes 1638400

commit v5 on v4

--- a/solution.py
+++ b/solution.py
@@ -133,7 +133,7 @@
         def step(i, carry):
             return body(pl.ds(pl.multiple_of(i * CHUNK, CHUNK), CHUNK), carry)
 
-        return lax.fori_loop(0, rows // CHUNK, step, start, unroll=2)
+        return lax.fori_loop(0, rows // CHUNK, step, start, unroll=5)
 
     def arrived(side, block, step):
         data, top = copies(side, block, step)
@@ -233,13 +233,18 @@
 
             @pl.when((turn == 0) & (step == 0))
             def _():
-                for k in range(1, Z_SIZE):
+                for k in (1, Z_SIZE - 1):
                     transpose_group((far_group + k) % Z_SIZE)
 
             @pl.when(step < half - 1)
             def _():
                 for side in range(2):
                     send_on(side, 1 - side, 2 * pair + 1 - side, step)
+
+            @pl.when((turn == 0) & (step == 0))
+            def _():
+                for k in range(2, Z_SIZE - 1):
+                    transpose_group((far_group + k) % Z_SIZE)
 
             @pl.when((step == 0) & (turn > 0))
             def _():
@@ -311,11 +316,11 @@
             coef_first, coef_second = coefs(*sums[3 * j : 3 * j + 3])
 
             def mix(part, carry):
-                mixed = coef_first * gathered[j, part, :] + coef_second * gathered[j + left, part, :]
+                terms = coef_first * gathered[j, part, :], coef_second * gathered[j + left, part, :]
                 if left == 1:
-                    out_ref[part, :] = mixed
+                    out_ref[0, part, :], out_ref[1, part, :] = terms
                 else:
-                    gathered[j, part, :] = mixed
+                    gathered[j, part, :] = terms[0] + terms[1]
 
             by_chunk(mix)
 
@@ -358,7 +363,8 @@
         def mix(part, carry):
             below = pairs[0][0] * gathered[0, part, :] + pairs[0][1] * gathered[2, part, :]
             above = pairs[1][0] * gathered[1, part, :] + pairs[1][1] * gathered[3, part, :]
-            out_ref[part, :] = low * below + high * above
+            out_ref[0, part, :] = low * below
+            out_ref[1, part, :] = high * above
 
         by_chunk(mix)
 
@@ -400,9 +406,9 @@
         lines = max(24, -(-3 * nodes // 2 // 8) * 8)
         hop = (2, nodes, half)
         dma = pltpu.SemaphoreType.DMA
-        return pl.pallas_call(
+        terms = pl.pallas_call(
             functools.partial(kernel, nodes, count),
-            out_shape=jax.ShapeDtypeStruct((rows, cols), jnp.float32),
+            out_shape=jax.ShapeDtypeStruct((2, rows, cols), jnp.float32),
             in_specs=[pl.BlockSpec(memory_space=pl.ANY)] * 2,
             out_specs=pl.BlockSpec(memory_space=pltpu.VMEM),
             scratch_shapes=[
@@ -427,6 +433,7 @@
             compiler_params=pltpu.CompilerParams(
                 collective_id=0, has_side_effects=True, vmem_limit_bytes=60 * 2**20),
         )(activations, grad_out)
+        return terms[0] + terms[1]
 
     in_specs = (P(("node", "fsdp"), None), P(("node", "fsdp"), None))
     return jax.shard_map(local, mesh=mesh, in_specs=in_specs, out_specs=P("fsdp", "node"), check_vma=False)

time: 150 us -> 150 us (level)
  other arithmetic: 0 us -> 2.37 us
  local copies, waits for them, and re-layouts: 2.09 us -> 0 us
    add x0 -> x1, other arithmetic: none -> 2.37 us  [local(): return terms[0] + terms[1]]
    unnamed x1 -> x0, local copies, waits for them, and re-layouts: 2.09 us -> none
where the time goes in v5:
time: 150 us
  Pallas kernels  148 us (99%)
  other arithmetic  2.37 us (2%)
    pallas_call x1, Pallas kernels, local(): pl.pallas_call(functools.partial(kernel, nodes, count), out_shape=jax.Sha...  148 us

profile of v5, /device:TPU:0, one launch (start us, length us, event | category | flops | bytes accessed | tf_op | source)
XLA Modules:
  0.0 149.9 jit_solution(10441948214613017262)
XLA Ops:
  0.0 147.6 %shard_map.28 = f32[2,320,640]{2,1,0:T(8,128)} custom-call(bf16[1024,2560]{1,0:T(8,128)(2,1)} %a_ref.1, bf16[1024,2560]{1,0:T(8,128)(2,1)} %g_hbm.1), custom_call_target="tpu_custom_call" | custom-call | tf_op jit(solution)/shard_map/pallas_call | solution.py:409
  147.6 2.4 %add_bitcast_fusion = f32[320,640]{1,0:T(8,128)} fusion(f32[2,320,640]{2,1,0:T(8,128)} %shard_map.28), kind=kLoop, calls=%fused_computation | loop fusion | flops 204800 | bytes 2457600 | tf_op jit(solution)/shard_map/add | solution.py:436

commit v6 on v5

--- a/solution.py
+++ b/solution.py
@@ -62,6 +62,8 @@
     node = lax.axis_index("node")
     place = lax.axis_index("fsdp")
     rows, cols = acc.shape
+    pieces = swap_send.shape[1]
+    size = rows // pieces
     me = ring_position(place, count)
     right = ring_place((me + 1) % count, count)
     left = ring_place((me + count - 1) % count, count)
@@ -129,11 +131,11 @@
             device_id=target, device_id_type=MESH)
         return data, top
 
-    def by_chunk(body, start=None):
+    def by_chunk(body, start=None, first=0, number=rows):
         def step(i, carry):
-            return body(pl.ds(pl.multiple_of(i * CHUNK, CHUNK), CHUNK), carry)
-
-        return lax.fori_loop(0, rows // CHUNK, step, start, unroll=5)
+            return body(pl.ds(pl.multiple_of(first + i * CHUNK, CHUNK), CHUNK), carry)
+
+        return lax.fori_loop(0, number // CHUNK, step, start, unroll=5)
 
     def arrived(side, block, step):
         data, top = copies(side, block, step)
@@ -178,10 +180,11 @@
         top.start()
         data.start()
 
-    def swap(block):
+    def swap(block, piece, sender):
+        part = pl.ds(pl.multiple_of(piece * size, 8), size)
         return pltpu.make_async_remote_copy(
-            src_ref=own.at[block], dst_ref=gathered.at[node],
-            send_sem=swap_send.at[block], recv_sem=swap_recv.at[node],
+            src_ref=own.at[block, part], dst_ref=gathered.at[sender, part],
+            send_sem=swap_send.at[block, piece], recv_sem=swap_recv.at[sender, piece],
             device_id=(block, place), device_id_type=MESH)
 
     def prepare(parity, block):
@@ -193,7 +196,7 @@
 
         by_chunk(add)
 
-    def finish(parity, block):
+    def finish(parity, block, send):
         top = arrived(parity, block, half - 1)
 
         def total(part):
@@ -204,8 +207,10 @@
             def store(part, carry):
                 own[block, part, :] = total(part)
 
-            by_chunk(store)
-            swap(block).start()
+            for piece in range(pieces):
+                by_chunk(store, None, piece * size, size)
+                if send:
+                    swap(block, piece, node).start()
 
         @pl.when(block == node)
         def _():
@@ -214,11 +219,11 @@
 
             by_chunk(store)
 
-    def finish_pair(turn):
+    def finish_pair(turn, send):
         for parity in range(2):
             prepare(parity, 2 * pair_at(turn) + parity)
         for parity in (1 - node % 2, node % 2):
-            finish(parity, 2 * pair_at(turn) + parity)
+            finish(parity, 2 * pair_at(turn) + parity, send)
 
     @pl.loop(0, nodes // 2)
     def _(turn):
@@ -248,19 +253,16 @@
 
             @pl.when((step == 0) & (turn > 0))
             def _():
-                finish_pair(turn - 1)
-
-    finish_pair(nodes // 2 - 1)
-
-    @pl.loop(1, nodes)
-    def _(k):
-        other = (node + k) % nodes
-        pltpu.make_async_remote_copy(
-            src_ref=own.at[other], dst_ref=gathered.at[other],
-            send_sem=swap_send.at[other], recv_sem=swap_recv.at[other],
-            device_id=(other, place), device_id_type=MESH).wait_recv()
-
-    def exchange(level, stage, size):
+                finish_pair(turn - 1, False)
+
+            @pl.when((turn > 0) & (step < pieces))
+            def _():
+                for parity in range(2):
+                    swap(2 * pair_at(turn - 1) + parity, step, node).start()
+
+    finish_pair(nodes // 2 - 1, True)
+
+    def exchange(level, stage, members):
         def copy(k):
             far = (node, (place + k) % count) if stage == 0 else ((node + k) % nodes, place)
             return pltpu.make_async_remote_copy(
@@ -268,13 +270,13 @@
                 send_sem=sum_send.at[level, stage, k], recv_sem=sum_recv.at[level, stage, k],
                 device_id=far, device_id_type=MESH)
 
-        for k in range(1, size):
+        for k in range(1, members):
             copy(k).start()
         total = sums_mine[level, stage]
-        for k in range(1, size):
+        for k in range(1, members):
             copy(k).wait_recv()
             total = total + sums_came[level, stage, k]
-        for k in range(1, size):
+        for k in range(1, members):
             copy(k).wait_send()
         return total
 
@@ -291,8 +293,15 @@
             part = pl.ds(pl.multiple_of(i * 8, 8), 8)
             return tuple(t + fold(a * b) for t, (a, b) in zip(sums, pairs_of(part)))
 
-        start = jnp.zeros((8, cols if cols % 128 else 128), jnp.float32)
-        sums = lax.fori_loop(0, rows // 8, step, (start,) * number, unroll=2)
+        sums = (jnp.zeros((8, cols if cols % 128 else 128), jnp.float32),) * number
+        for piece in range(pieces):
+            if level == 0:
+                @pl.loop(1, nodes)
+                def _(k):
+                    other = (node + k) % nodes
+                    swap(other, piece, other).wait_recv()
+
+            sums = lax.fori_loop(piece * size // 8, (piece + 1) * size // 8, step, sums, unroll=2)
         tile = jnp.zeros(sums_mine.shape[2:], jnp.float32)
         line = lax.broadcasted_iota(jnp.int32, tile.shape, 0)
         for i, term in enumerate(sums):
@@ -379,7 +388,8 @@
 
     @pl.loop(1, nodes)
     def _(k):
-        swap((node + k) % nodes).wait_send()
+        for piece in range(pieces):
+            swap((node + k) % nodes, piece, node).wait_send()
 
     @pl.loop(0, nodes // 2)
     def _(pair):
@@ -405,6 +415,7 @@
             grad_out = grad_out.reshape(tokens, nodes, cols).transpose(1, 0, 2)
         lines = max(24, -(-3 * nodes // 2 // 8) * 8)
         hop = (2, nodes, half)
+        pieces = 2 if rows % (4 * CHUNK) else 4
         dma = pltpu.SemaphoreType.DMA
         terms = pl.pallas_call(
             functools.partial(kernel, nodes, count),
@@ -427,7 +438,7 @@
                 pltpu.VMEM((levels, 2, max(nodes, count), lines, 128), jnp.float32),
                 dma((Z_SIZE,)), dma((nodes,)),
                 dma(hop), dma(hop), dma(hop), dma(hop),
-                dma((nodes,)), dma((nodes,)),
+                dma((nodes, pieces)), dma((nodes, pieces)),
                 dma((levels, 2, max(nodes, count))), dma((levels, 2, max(nodes, count))),
             ],
             compiler_params=pltpu.CompilerParams(

time: 150 us -> 150 us (level)
  no operation moved by 1% of the time
where the time goes in v6:
time: 150 us
  Pallas kernels  148 us (99%)
  other arithmetic  2.37 us (2%)
    pallas_call x1, Pallas kernels, local(): pl.pallas_call(functools.partial(kernel, nodes, count), out_shape=jax.Sha...  148 us

profile of v6, /device:TPU:0, one launch (start us, length us, event | category | flops | bytes accessed | tf_op | source)
XLA Modules:
  0.0 150.2 jit_solution(6792974036940511810)
XLA Ops:
  0.0 147.8 %shard_map.28 = f32[2,320,640]{2,1,0:T(8,128)} custom-call(bf16[1024,2560]{1,0:T(8,128)(2,1)} %a_ref.1, bf16[1024,2560]{1,0:T(8,128)(2,1)} %g_hbm.1), custom_call_target="tpu_custom_call" | custom-call | tf_op jit(solution)/shard_map/pallas_call | solution.py:420
  147.8 2.4 %add_bitcast_fusion = f32[320,640]{1,0:T(8,128)} fusion(f32[2,320,640]{2,1,0:T(8,128)} %shard_map.28), kind=kLoop, calls=%fused_computation | loop fusion | flops 204800 | bytes 2457600 | tf_op jit(solution)/shard_map/add | solution.py:447

commit v7 on v6

--- a/solution.py
+++ b/solution.py
@@ -56,8 +56,8 @@
 
 def kernel(
     nodes, count, a_ref, g_hbm, out_ref,
-    raw, at_ref, g_ref, sent, came, sent_top, came_top, acc, peaks, own, gathered, sums_mine, sums_came,
-    a_sem, g_sem, send_sem, recv_sem, top_send, top_recv, swap_send, swap_recv, sum_send, sum_recv,
+    raw, at_ref, g_ref, sent, came, acc, peaks, own, gathered, sums_mine, sums_came,
+    a_sem, g_sem, send_sem, recv_sem, swap_send, swap_recv, sum_send, sum_recv,
 ):
     node = lax.axis_index("node")
     place = lax.axis_index("fsdp")
@@ -119,17 +119,22 @@
         mine = at_ref[pl.ds(pl.multiple_of(owner * rows, 16), rows), :]
         acc[...] = jnp.dot(mine, g_view(g_ref, block)[...], preferred_element_type=jnp.float32)
 
-    def copies(side, block, step):
-        target = (node, right * (1 - side) + left * side)
-        data = pltpu.make_async_remote_copy(
+    wide = sent.shape[-1]
+    slabs = cols // wide
+    tail = pl.ds(slabs * rows, 16)
+
+    def hop_copy(side, block, step):
+        return pltpu.make_async_remote_copy(
             src_ref=sent.at[side, block, step], dst_ref=came.at[side, block, step],
             send_sem=send_sem.at[side, block, step], recv_sem=recv_sem.at[side, block, step],
-            device_id=target, device_id_type=MESH)
-        top = pltpu.make_async_remote_copy(
-            src_ref=sent_top.at[side, block, step], dst_ref=came_top.at[side, block, step],
-            send_sem=top_send.at[side, block, step], recv_sem=top_recv.at[side, block, step],
-            device_id=target, device_id_type=MESH)
-        return data, top
+            device_id=(node, right * (1 - side) + left * side), device_id_type=MESH)
+
+    def slab(part, i):
+        return pl.ds(pl.multiple_of(part.start + i * rows, CHUNK), CHUNK)
+
+    def received(side, block, step, part, top):
+        codes = [came[side, block, step, slab(part, i), :] for i in range(slabs)]
+        return decode(jnp.concatenate(codes, axis=1), top)
 
     def by_chunk(body, start=None, first=0, number=rows):
         def step(i, carry):
@@ -138,10 +143,8 @@
         return lax.fori_loop(0, number // CHUNK, step, start, unroll=5)
 
     def arrived(side, block, step):
-        data, top = copies(side, block, step)
-        top.wait_recv()
-        data.wait_recv()
-        return came_top[side, block, step][0:1, 0:1].astype(jnp.float32)
+        hop_copy(side, block, step).wait_recv()
+        return came[side, block, step, tail, :][0:1, 0:1].astype(jnp.float32)
 
     def hops(side, parity):
         return half if side == parity else count - 1 - half
@@ -156,7 +159,7 @@
             top = arrived(side, block, step - 1)
 
             def add(part, peak):
-                value = acc[part, :] + decode(came[side, block, step - 1, part, :], top)
+                value = acc[part, :] + received(side, block, step - 1, part, top)
                 acc[part, :] = value
                 return jnp.maximum(peak, jnp.abs(value))
 
@@ -168,17 +171,17 @@
                 lambda part, peak: jnp.maximum(peak, jnp.abs(acc[part, :])), jnp.zeros(peaks.shape, jnp.float32))
 
         largest = jnp.maximum(jnp.max(peaks[...], axis=(0, 1), keepdims=True), 1e-30)
-        tile = jnp.broadcast_to(largest, (16, 128)).astype(jnp.bfloat16)
-        sent_top[side, block, step] = tile
+        tile = jnp.broadcast_to(largest, (16, wide)).astype(jnp.bfloat16)
+        sent[side, block, step, tail, :] = tile
         scale = TOP / tile[0:1, 0:1].astype(jnp.float32)
 
         def code(part, carry):
-            sent[side, block, step, part, :] = encode(acc[part, :], scale)
+            codes = encode(acc[part, :], scale)
+            for i in range(slabs):
+                sent[side, block, step, slab(part, i), :] = codes[:, i * wide : (i + 1) * wide]
 
         by_chunk(code)
-        data, top = copies(side, block, step)
-        top.start()
-        data.start()
+        hop_copy(side, block, step).start()
 
     def swap(block, piece, sender):
         part = pl.ds(pl.multiple_of(piece * size, 8), size)
@@ -192,15 +195,15 @@
         top = arrived(1 - parity, block, half - 2)
 
         def add(part, carry):
-            own[block, part, :] = acc[part, :] + decode(came[1 - parity, block, half - 2, part, :], top)
+            own[block, part, :] = acc[part, :] + received(1 - parity, block, half - 2, part, top)
 
         by_chunk(add)
 
-    def finish(parity, block, send):
+    def finish(parity, block):
         top = arrived(parity, block, half - 1)
 
         def total(part):
-            return own[block, part, :] + decode(came[parity, block, half - 1, part, :], top)
+            return own[block, part, :] + received(parity, block, half - 1, part, top)
 
         @pl.when(block != node)
         def _():
@@ -209,8 +212,7 @@
 
             for piece in range(pieces):
                 by_chunk(store, None, piece * size, size)
-                if send:
-                    swap(block, piece, node).start()
+                swap(block, piece, node).start()
 
         @pl.when(block == node)
         def _():
@@ -219,11 +221,11 @@
 
             by_chunk(store)
 
-    def finish_pair(turn, send):
+    def finish_pair(turn):
         for parity in range(2):
             prepare(parity, 2 * pair_at(turn) + parity)
         for parity in (1 - node % 2, node % 2):
-            finish(parity, 2 * pair_at(turn) + parity, send)
+            finish(parity, 2 * pair_at(turn) + parity)
 
     @pl.loop(0, nodes // 2)
     def _(turn):
@@ -253,14 +255,9 @@
 
             @pl.when((step == 0) & (turn > 0))
             def _():
-                finish_pair(turn - 1, False)
-
-            @pl.when((turn > 0) & (step < pieces))
-            def _():
-                for parity in range(2):
-                    swap(2 * pair_at(turn - 1) + parity, step, node).start()
-
-    finish_pair(nodes // 2 - 1, True)
+                finish_pair(turn - 1)
+
+    finish_pair(nodes // 2 - 1)
 
     def exchange(level, stage, members):
         def copy(k):
@@ -397,9 +394,7 @@
             for side in range(2):
                 @pl.loop(0, hops(side, parity))
                 def _(step):
-                    data, top = copies(side, 2 * pair + parity, step)
-                    top.wait_send()
-                    data.wait_send()
+                    hop_copy(side, 2 * pair + parity, step).wait_send()
 
 
 def solution(mesh):
@@ -415,6 +410,7 @@
             grad_out = grad_out.reshape(tokens, nodes, cols).transpose(1, 0, 2)
         lines = max(24, -(-3 * nodes // 2 // 8) * 8)
         hop = (2, nodes, half)
+        wide = cols if cols % 128 else 128
         pieces = 2 if rows % (4 * CHUNK) else 4
         dma = pltpu.SemaphoreType.DMA
         terms = pl.pallas_call(
@@ -426,10 +422,8 @@
                 pltpu.VMEM((tokens, features), jnp.bfloat16),
                 pltpu.VMEM((features, tokens), jnp.bfloat16),
                 pltpu.VMEM(grad_out.shape, jnp.bfloat16),
-                pltpu.VMEM(hop + (rows, cols), jnp.bfloat16),
-                pltpu.VMEM(hop + (rows, cols), jnp.bfloat16),
-                pltpu.VMEM(hop + (16, 128), jnp.bfloat16),
-                pltpu.VMEM(hop + (16, 128), jnp.bfloat16),
+                pltpu.VMEM(hop + (cols // wide * rows + 16, wide), jnp.bfloat16),
+                pltpu.VMEM(hop + (cols // wide * rows + 16, wide), jnp.bfloat16),
                 pltpu.VMEM((rows, cols), jnp.float32),
                 pltpu.VMEM((CHUNK, cols), jnp.float32),
                 pltpu.VMEM((nodes, rows, cols), jnp.float32),
@@ -437,7 +431,7 @@
                 pltpu.VMEM((levels, 2, lines, 128), jnp.float32),
                 pltpu.VMEM((levels, 2, max(nodes, count), lines, 128), jnp.float32),
                 dma((Z_SIZE,)), dma((nodes,)),
-                dma(hop), dma(hop), dma(hop), dma(hop),
+                dma(hop), dma(hop),
                 dma((nodes, pieces)), dma((nodes, pieces)),
                 dma((levels, 2, max(nodes, count))), dma((levels, 2, max(nodes, count))),
             ],

time: 150 us -> 150 us (level)
  no operation moved by 1% of the time
where the time goes in v7:
time: 150 us
  Pallas kernels  147 us (98%)
  other arithmetic  2.37 us (2%)
    pallas_call x1, Pallas kernels, local(): pl.pallas_call(functools.partial(kernel, nodes, count), out_shape=jax.Sha...  147 us

profile of v7, /device:TPU:0, one launch (start us, length us, event | category | flops | bytes accessed | tf_op | source)
XLA Modules:
  0.0 149.6 jit_solution(6971776513401660534)
XLA Ops:
  0.0 147.2 %shard_map.28 = f32[2,320,640]{2,1,0:T(8,128)} custom-call(bf16[1024,2560]{1,0:T(8,128)(2,1)} %a_ref.1, bf16[1024,2560]{1,0:T(8,128)(2,1)} %g_hbm.1), custom_call_target="tpu_custom_call" | custom-call | tf_op jit(solution)/shard_map/pallas_call | solution.py:416
  147.2 2.4 %add_bitcast_fusion = f32[320,640]{1,0:T(8,128)} fusion(f32[2,320,640]{2,1,0:T(8,128)} %shard_map.28), kind=kLoop, calls=%fused_computation | loop fusion | flops 204800 | bytes 2457600 | tf_op jit(solution)/shard_map/add | solution.py:441
